TPU v7x, 32 devices: a whole 2x2x4 slice. The times are simulated.
32 devices in a mesh: groups: 2 (over y), var: 8 (over z, x), tm: 2 (over core).
Axes of the slice: x: 2, y: 2, z: 4, core: 2. Of those that a mesh axis runs over, the one named last changes fastest.
Arguments:
- series: bfloat16 [4, 512, 4096], P('groups', 'var', 'tm'), parts along dimension 0, may hold values from -71 to 71
- target: float32 [4, 512, 720], P('groups', 'var', 'tm'), parts along dimension 0, may hold values from -71 to 71
- w_embed: bfloat16 [4096, 512], P('tm'), may hold values from -0.09375 to 0.09375
- w_query: bfloat16 [512, 256], P(None, 'tm'), may hold values from -0.25 to 0.25
- w_key: bfloat16 [512, 256], P(None, 'tm'), may hold values from -0.25 to 0.25
- w_value: bfloat16 [512, 256], P(None, 'tm'), may hold values from -0.25 to 0.25
- w_out: bfloat16 [256, 512], P('tm'), may hold values from -0.375 to 0.375
- norm_gain: float32 [512], replicated, may hold values from 0.5 to 1.5
- w_head: bfloat16 [512, 720], P(None, 'tm'), may hold values from -0.25 to 0.25
Outputs:
- predicted_values: float32 [4, 512, 720], P('groups', 'var', 'tm'), parts along dimension 0
- question_projection_derivative: float32 [1024, 256], P('groups', 'tm'), parts along dimension 0
- final_projection_derivative: float32 [512, 512], P(('groups', 'tm')), parts along dimension 0
- layernorm_scale_derivative: float32 [1024], P('groups'), parts along dimension 0
- future_readout_derivative: float32 [1024, 720], P('groups', 'tm'), parts along dimension 0
There are 2 independent parts, one for each index of `groups`. A program takes and returns all parts, laid end to end along the dimension named above; an argument that names none is the same for every part. Nothing has to cross between parts.
All inputs are finite; a program needn't handle non-finite values.
Results may differ from a plain program's by a relative error of at most 0.015.
Values may be sent and summed in bfloat16 or wider, within the bound.
A program may use at most 128 MiB of HBM per device.

v0:
```python
import jax
import jax.numpy as jnp
from jax import lax
from jax.sharding import PartitionSpec as P

HEAD_DIM = 64
HOR = 720
SAMPLES = 2


epsilon = 1e-05


def split_heads(tensor_in):
    return tensor_in.reshape(tensor_in.shape[:-1] + (tensor_in.shape[-1] // HEAD_DIM, HEAD_DIM))


def project(inputs, matrix):
    return jnp.einsum("svd,da->sva", inputs, matrix, preferred_element_type=jnp.float32).astype(
        jnp.bfloat16
    )


def forward_attend(queries, key_rows, value_rows):
    scores = jnp.einsum(
        "nhe,mhe->hnm", queries, key_rows, preferred_element_type=jnp.float32
    ) * HEAD_DIM ** (-0.5)
    powers = jnp.exp(scores)
    row_sums = jnp.sum(powers, axis=2)
    summed = jnp.einsum(
        "hnm,mhe->nhe", powers.astype(jnp.bfloat16), value_rows, preferred_element_type=jnp.float32
    )
    return (summed / jnp.transpose(row_sums)[:, :, None], row_sums)


def attend_all(queries, key_rows, value_rows):
    contexts = []
    totals = []
    for sample in range(queries.shape[0]):
        context, row_sums = forward_attend(
            split_heads(queries[sample]),
            split_heads(key_rows[sample]),
            split_heads(value_rows[sample]),
        )
        contexts.append(context.reshape(queries.shape[1], queries.shape[2]))
        totals.append(row_sums)
    return (jnp.stack(contexts), totals)


def backward_attend(queries, key_rows, value_rows, row_sums, context, grad_context):
    scores = jnp.einsum(
        "nhe,mhe->hnm", queries, key_rows, preferred_element_type=jnp.float32
    ) * HEAD_DIM ** (-0.5)
    weights = jnp.exp(scores) / row_sums[:, :, None]
    grad_weights = jnp.einsum(
        "nhe,mhe->hnm",
        grad_context.astype(jnp.bfloat16),
        value_rows,
        preferred_element_type=jnp.float32,
    )
    row_dots = jnp.sum(grad_context * context, axis=2)
    grad_scores = (weights * (grad_weights - jnp.transpose(row_dots)[:, :, None])).astype(
        jnp.bfloat16
    )
    return jnp.einsum(
        "hnm,mhe->nhe", grad_scores, key_rows, preferred_element_type=jnp.float32
    ) * HEAD_DIM ** (-0.5)


def backward_all(queries, key_rows, value_rows, totals, context, grad_context):
    results = []
    for sample in range(queries.shape[0]):
        grad_rows = backward_attend(
            split_heads(queries[sample]),
            split_heads(key_rows[sample]),
            split_heads(value_rows[sample]),
            totals[sample],
            split_heads(context[sample]),
            split_heads(grad_context[sample]),
        )
        results.append(grad_rows.reshape(queries.shape[1], queries.shape[2]))
    return jnp.stack(results).astype(jnp.bfloat16)


def per_device(series, target, w_embed, w_query, w_key, w_value, w_out, norm_gain, w_head):
    samples, var_rows, steps_local = series.shape
    look_total = steps_local * lax.axis_size("tm")
    series_f = series.astype(jnp.float32)
    level_sum, square_sum = lax.psum(
        (jnp.sum(series_f, axis=2), jnp.sum(series_f * series_f, axis=2)), "tm"
    )
    instance_average = level_sum / look_total
    spread = square_sum / look_total - instance_average * instance_average
    centered = series_f - instance_average[:, :, None]
    instance_dispersion = jnp.sqrt(spread + epsilon)
    normed = (centered / instance_dispersion[:, :, None]).astype(jnp.bfloat16)
    partial_embed = jnp.einsum("svl,ld->svd", normed, w_embed, preferred_element_type=jnp.float32)
    hidden = lax.psum(partial_embed, "tm").astype(jnp.bfloat16)
    queries = project(hidden, w_query)
    key_rows = project(hidden, w_key)
    value_rows = project(hidden, w_value)
    all_keys, all_values = (
        lax.all_gather(key_rows, "var", axis=1, tiled=True),
        lax.all_gather(value_rows, "var", axis=1, tiled=True),
    )
    context, totals = attend_all(queries, all_keys, all_values)
    context_low = context.astype(jnp.bfloat16)
    mixing = lax.psum(
        jnp.einsum("sva,ad->svd", context_low, w_out, preferred_element_type=jnp.float32).astype(
            jnp.bfloat16
        ),
        "tm",
    ).astype(jnp.float32)
    residual = hidden.astype(jnp.float32) + mixing
    shifted = residual - jnp.mean(residual, axis=2, keepdims=True)
    norm_root = jnp.sqrt(jnp.mean(shifted * shifted, axis=2, keepdims=True) + epsilon)
    unit_rows = shifted / norm_root
    normal_out = (unit_rows * norm_gain).astype(jnp.bfloat16)
    future_rescaler = jnp.einsum(
        "svd,dh->svh", normal_out, w_head, preferred_element_type=jnp.float32
    )
    predicted_values = (
        future_rescaler * instance_dispersion[:, :, None] + instance_average[:, :, None]
    )
    errors = (
        future_rescaler - (target - instance_average[:, :, None]) / instance_dispersion[:, :, None]
    )
    grad_horizon = (errors * (2.0 / (SAMPLES * HOR))).astype(jnp.bfloat16)
    head_term = jnp.einsum(
        "svd,svh->dh", normal_out, grad_horizon, preferred_element_type=jnp.float32
    )
    grad_normal = lax.psum(
        jnp.einsum("svh,dh->svd", grad_horizon, w_head, preferred_element_type=jnp.float32).astype(
            jnp.bfloat16
        ),
        "tm",
    ).astype(jnp.float32)
    gain_term = jnp.sum(grad_normal * unit_rows, axis=(0, 1))
    grad_unit = grad_normal * norm_gain
    grad_mix = (
        (
            grad_unit
            - jnp.mean(grad_unit, axis=2, keepdims=True)
            - unit_rows * jnp.mean(grad_unit * unit_rows, axis=2, keepdims=True)
        )
        / norm_root
    ).astype(jnp.bfloat16)
    out_term = jnp.einsum("sva,svd->da", context_low, grad_mix, preferred_element_type=jnp.float32)
    grad_context = jnp.einsum("svd,ad->sva", grad_mix, w_out, preferred_element_type=jnp.float32)
    grad_query = backward_all(queries, all_keys, all_values, totals, context, grad_context)
    query_term = jnp.einsum("svd,sva->da", hidden, grad_query, preferred_element_type=jnp.float32)
    future_readout_derivative, gain_gradient_total, output_gradient_total, query_gradient_total = (
        lax.psum((head_term, gain_term, out_term, query_term), "var")
    )
    return (
        predicted_values,
        query_gradient_total,
        jnp.transpose(output_gradient_total),
        gain_gradient_total,
        future_readout_derivative,
    )


def solution(mesh):
    in_specs = (
        P("groups", "var", "tm"),
        P("groups", "var", "tm"),
        P("tm", None),
        P(None, "tm"),
        P(None, "tm"),
        P(None, "tm"),
        P("tm", None),
        P(),
        P(None, "tm"),
    )
    out_specs = (
        P("groups", "var", "tm"),
        P("groups", "tm"),
        P(("groups", "tm"), None),
        P("groups"),
        P("groups", "tm"),
    )
    return jax.shard_map(
        per_device, mesh=mesh, in_specs=in_specs, out_specs=out_specs, check_vma=False
    )
```

profile of v0, /device:TPU:0, one launch (start us, length us, event | category | flops | bytes accessed | tf_op | source)
XLA Modules:
  0.0 234.3 jit_solution(17725710917691183952)
XLA Ops:
  7.2 1.4 convert_reduce_fusion
  8.6 2.6 %all-reduce.1 = (f32[2,64]{1,0:T(2,128)S(1)}, f32[2,64]{1,0:T(2,128)S(1)}) all-reduce(f32[2,64]{1,0:T(2,128)S(1)} %get-tuple-element.6, f32[2,64]{1,0:T(2,128)S(1)} %get-tuple-element.5), channel_id=1, replica_groups=mesh['groups'=2,'var'=8,'tm'=2] {'tm'}, use_global_device_ids=true, to_apply=%region_3.0 | all-reduce | flops 256 | bytes 2048 | tf_op jit(solution)/shard_map/psum | solution.py:89
  11.2 0.6 copy-done.16
  11.8 1.6 fusion
  13.4 4.4 %all-reduce.12 = bf16[2,64,512]{2,1,0:T(8,128)(2,1)S(1)} all-reduce(f32[2,64,512]{2,1,0:T(8,128)S(1)} %fusion), channel_id=1, replica_groups=mesh['groups'=2,'var'=8,'tm'=2] {'tm'}, use_global_device_ids=true, to_apply=%region_4.0 | all-reduce | flops 65536 | bytes 393216 | tf_op jit(solution)/shard_map/psum | solution.py:98
  17.8 0.2 convolution_convert_fusion.2
  18.0 0.2 convolution_convert_fusion.3
  18.2 0.1 reshape_squeeze.31
  18.3 0.1 reshape_squeeze.34
  18.3 0.2 convolution_convert_fusion.4
  18.5 32.3 %all_gather.6 = bf16[2,512,128]{2,1,0:T(8,128)(2,1)S(1)} all-gather(bf16[2,64,128]{2,1,0:T(8,128)(2,1)S(1)} %convolution_convert_fusion.4), channel_id=1, replica_groups=mesh['groups'=2,'var'=8,'tm'=2] {'var'}, dimensions={1}, use_global_device_ids=true | all-gather | bytes 294912 | tf_op jit(solution)/shard_map/all_gather | solution.py:104
  50.9 0.1 copy.28
  51.0 0.1 copy.31
  51.1 30.7 %all_gather.7 = bf16[2,512,128]{2,1,0:T(8,128)(2,1)S(1)} all-gather(bf16[2,64,128]{2,1,0:T(8,128)(2,1)S(1)} %convolution_convert_fusion.2), channel_id=1, replica_groups=mesh['groups'=2,'var'=8,'tm'=2] {'var'}, dimensions={1}, use_global_device_ids=true | all-gather | bytes 294912 | tf_op jit(solution)/shard_map/all_gather | solution.py:103
  81.9 0.1 copy.29
  82.0 0.1 copy.32
  82.1 0.3 fusion.68
  82.4 0.8 fusion.69
  83.2 0.1 copy.35
  83.3 0.3 fusion.70
  83.5 0.8 fusion.71
  84.3 0.1 copy.34
  84.5 0.8 convolution_convert_fusion.1
  85.4 18.9 %all-reduce.7.cloned.1.call-done = bf16[2,64,512]{2,1,0:T(8,128)(2,1)} async-done(((bf16[2,64,512]{2,1,0:T(8,128)(2,1)}), bf16[2,64,512]{2,1,0:T(8,128)(2,1)}) %all-reduce.7.cloned.1.call-update) | async-done | bytes 131088 | tf_op jit(solution)/shard_map/psum | solution.py:108
  104.3 1.1 fusion.36
  105.4 1.1 multiply_reduce_fusion
  106.5 2.2 multiply_convert_fusion.1
  108.7 0.6 copy-done.9
  109.3 0.9 convolution_convert_fusion
  110.3 2.1 convolution_bitcast_fusion
  112.4 17.0 %all-reduce.9.cloned.1.call-done = bf16[2,64,512]{2,1,0:T(8,128)(2,1)} async-done(((bf16[2,64,512]{2,1,0:T(8,128)(2,1)}), bf16[2,64,512]{2,1,0:T(8,128)(2,1)}) %all-reduce.9.cloned.1.call-update) | async-done | bytes 131088 | tf_op jit(solution)/shard_map/psum | solution.py:132
  129.5 1.7 fusion.31
  131.2 1.1 fusion.34
  132.3 0.2 fusion.38
  132.5 1.6 convolution_bitcast_fusion.1
  134.1 0.1 copy.36
  134.2 0.9 multiply_reduce_fusion.2
  135.1 1.1 fusion.15
  136.2 0.1 copy.38
  136.3 0.1 copy.37
  136.4 0.4 fusion.14
  136.8 0.1 copy.39
  136.9 0.9 convolution_bitcast_fusion.2
  137.9 22.8 %psum.70 = f32[512]{0:T(512)} all-reduce(f32[512]{0:T(512)S(1)} %copy-done.12), channel_id=1, replica_groups=mesh['groups'=2,'var'=8,'tm'=2] {'var'}, use_global_device_ids=true, to_apply=%region_18.0 | all-reduce | flops 512 | bytes 4096 | tf_op jit(solution)/shard_map/psum | solution.py:153
  160.6 61.8 %all-reduce.11.cloned.1.call-done = (f32[512,128]{1,0:T(8,128)}, f32[128,512]{1,0:T(8,128)}, f32[512,360]{0,1:T(8,128)}) async-done(((f32[512,128]{1,0:T(8,128)}, f32[128,512]{1,0:T(8,128)}, f32[512,360]{0,1:T(8,128)}), (f32[512,128]{1,0:T(8,128)}, f32[128,512]{1,0:T(8,128)}, f32[512,360]{0,1:T(8,128)})) %all-reduce.11.cloned.1.call-update) | async-done | bytes 1261584 | tf_op jit(solution)/shard_map/psum | solution.py:153
  222.4 1.7 copy.55
  224.0 1.7 copy.56
  225.7 2.0 copy.57
  (49 shorter events, 0.4 us)
Async XLA Ops:
  7.2 4.6 %copy-start = (bf16[2048,512]{1,0:T(8,128)(2,1)S(1)}, bf16[2048,512]{1,0:T(8,128)(2,1)}, u32[]{:S(2)}) copy-start(bf16[2048,512]{1,0:T(8,128)(2,1)} %param.11) | copy-start | bytes 6291460
  7.2 97.1 %all-reduce.7.cloned.1.call-start = ((), (), s32[]{:S(2)}) async-start(), calls=%async_computation | async-start | bytes 262144 | tf_op jit(solution)/shard_map/psum | solution.py:108
  11.2 0.6 copy-start.16
  11.2 0.6 copy-start.17
  11.8 6.0 %copy-start.6 = (bf16[512,128]{1,0:T(8,128)(2,1)S(1)}, bf16[512,128]{1,0:T(8,128)(2,1)}, u32[]{:S(2)}) copy-start(bf16[512,128]{1,0:T(8,128)(2,1)} %param.13) | copy-start | bytes 393220
  11.8 6.2 %copy-start.7 = (bf16[512,128]{1,0:T(8,128)(2,1)S(1)}, bf16[512,128]{1,0:T(8,128)(2,1)}, u32[]{:S(2)}) copy-start(bf16[512,128]{1,0:T(8,128)(2,1)} %param.12) | copy-start | bytes 393220
  11.8 6.5 %copy-start.8 = (bf16[512,128]{1,0:T(8,128)(2,1)S(1)}, bf16[512,128]{1,0:T(8,128)(2,1)}, u32[]{:S(2)}) copy-start(bf16[512,128]{1,0:T(8,128)(2,1)} %param.14) | copy-start | bytes 393220
  50.8 33.6 %copy-start.2 = (bf16[128,512]{1,0:T(8,128)(2,1)S(1)}, bf16[128,512]{1,0:T(8,128)(2,1)}, u32[]{:S(2)}) copy-start(bf16[128,512]{1,0:T(8,128)(2,1)} %param.15) | copy-start | bytes 393220
  82.4 0.9 copy-start.13
  83.5 1.8 copy-start.15
  84.4 0.9 copy-start.5
  85.3 44.2 %all-reduce.9.cloned.1.call-start = ((), (), s32[]{:S(2)}) async-start(), calls=%async_computation.1 | async-start | bytes 262144 | tf_op jit(solution)/shard_map/psum | solution.py:132
  104.3 5.0 %copy-start.3 = (bf16[512,360]{0,1:T(8,128)(2,1)S(1)}, bf16[512,360]{0,1:T(8,128)(2,1)}, u32[]{:S(2)}) copy-start(bf16[512,360]{0,1:T(8,128)(2,1)} %param.17) | copy-start | bytes 1105924
  104.3 6.0 %copy-start.1 = (bf16[2,64,512]{2,1,0:T(8,128)(2,1)S(1)}, bf16[2,64,512]{2,1,0:T(8,128)(2,1)}, u32[]{:S(2)}) copy-start(bf16[2,64,512]{2,1,0:T(8,128)(2,1)} %all-reduce.7.cloned.1.call-done) | copy-start | bytes 393220
  105.4 1.1 copy-start.10
  106.5 2.2 copy-start.11
  108.7 0.6 copy-start.9
  110.2 112.1 %all-reduce.11.cloned.1.call-start = ((), (), s32[]{:S(2)}) async-start(), calls=%async_computation.2 | async-start | bytes 2523136 | tf_op jit(solution)/shard_map/psum | solution.py:153
  132.3 4.1 %copy-start.4 = (f32[64,2,64]{0,2,1:T(8,128)S(1)}, f32[64,2,64]{0,2,1:T(8,128)}, u32[]{:S(2)}) copy-start(f32[64,2,64]{0,2,1:T(8,128)} %get-tuple-element.30) | copy-start | bytes 98308
  132.3 4.1 %copy-start.14 = (f32[2,64]{1,0:T(2,128)S(1)}, f32[2,64]{1,0:T(2,128)}, u32[]{:S(2)}) copy-start(f32[2,64]{1,0:T(2,128)} %copy-done.13) | copy-start | bytes 1540
  135.1 2.8 %copy-start.12 = (f32[512]{0:T(512)S(1)}, f32[512]{0:T(512)}, u32[]{:S(2)}) copy-start(f32[512]{0:T(512)} %get-tuple-element.7) | copy-start | bytes 6148
Sparse Core Ops, SparseCore 0:
  85.4 18.8 all-reduce.6
  110.4 19.0 all-reduce.8
  138.0 84.3 all-reduce.10
where the time goes:
time: 235 us; the launch traced here: 234 us
  waiting for transfers between devices  97.8 us (42%)
  blocking collectives  92.8 us (39%)
  matrix products  14.4 us (6%)
  between operations  14.1 us (6%)
  local copies, waits for them, and re-layouts  7.82 us (3%)
  other arithmetic  7.29 us (3%)
    psum x1, waiting for transfers between devices, per_device(): lax.psum((head_term, gain_term, out_term, query_term), 'var')  61.8 us
    all_gather x1, blocking collectives, per_device(): lax.all_gather(value_rows, 'var', axis=1, tiled=True)  32.3 us
    all_gather x1, blocking collectives, per_device(): lax.all_gather(key_rows, 'var', axis=1, tiled=True)  30.7 us
    psum x1, blocking collectives, per_device(): lax.psum((head_term, gain_term, out_term, query_term), 'var')  22.8 us
    psum x1, waiting for transfers between devices, per_device(): lax.psum(jnp.einsum('sva,ad->svd', context_low, w_out, preferred_element_...  18.9 us
    psum x1, waiting for transfers between devices, per_device(): lax.psum(jnp.einsum('svh,dh->svd', grad_horizon, w_head, preferred_elemen...  17 us
    unnamed x39, local copies, waits for them, and re-layouts  6.63 us
  transfers between devices with their start and end apart: 3, of which 3 were waited for; matrix products, arithmetic and copies ran while one was open for 1% of the time, Pallas kernels for 0%

commit v1 on v0

v1 whole, which is shorter than its diff:
```python
import functools

import jax
import jax.numpy as jnp
from jax import lax
from jax.experimental import pallas as pl
from jax.experimental.pallas import tpu as pltpu
from jax.sharding import PartitionSpec as P

HEAD_DIM = 64
EPSILON = 1e-05
MESH = pl.DeviceIdType.MESH
F32, BF16 = jnp.float32, jnp.bfloat16


def dot(a, b):
    return jnp.dot(a, b, preferred_element_type=F32)


def dot_nt(a, b):
    return lax.dot_general(a, b, (((1,), (1,)), ((), ())), preferred_element_type=F32)


def dot_tn(a, b):
    return lax.dot_general(a, b, (((0,), (0,)), ((), ())), preferred_element_type=F32)


def repeat(count, body, carry):
    if count == 1:
        return body(0, carry)
    return lax.fori_loop(0, count, body, carry)


def kernel(
    n, reduce_here, key_chunk,
    series, target, w_embed, w_query, w_key, w_value, w_out, norm_gain, w_head,
    pred_out, query_out, final_out, gain_out, head_out,
    pack, got, wq, wk, wv, wo, wh, tg, hid, keys, values, powers, pred_half, pred_got,
    no2, gh_all, gh2, gm2, cl_all, cl2, gq_src, gq_all, gains, gain_mine,
    head_src, head_slots, head_full, out_src, out_slots, out_full,
    pair_send, pair_recv, hid_send, hid_recv, gq_send, gq_recv, gain_send, gain_recv,
    hr_send, hr_recv, ha_send, ha_recv, or_send, or_recv, oa_send, oa_recv,
):
    me = lax.axis_index("var")
    t = lax.axis_index("tm")
    other = 1 - t
    my_id = me * 2 + t
    rows = series.shape[1]
    steps = series.shape[2]
    horizon = 2 * target.shape[2]
    samples = series.shape[0]
    heads_half = w_query.shape[1] // HEAD_DIM
    heads = 2 * heads_half
    block = pl.ds(pl.multiple_of(me * rows, rows), rows)

    def to_pair(index, src, dst):
        return pltpu.make_async_remote_copy(
            src_ref=src, dst_ref=dst, send_sem=pair_send.at[index], recv_sem=pair_recv.at[index],
            device_id={"var": me, "tm": other}, device_id_type=MESH,
        )

    def spread(src_of, dst_of, send, recv):
        def go(i, carry):
            peer = lax.rem(me + 1 + i, n)
            pltpu.make_async_remote_copy(
                src_ref=src_of(peer), dst_ref=dst_of(me), send_sem=send.at[peer], recv_sem=recv.at[me],
                device_id={"var": peer, "tm": t}, device_id_type=MESH,
            ).start()
            return carry
        lax.fori_loop(0, n - 1, go, 0)

    def settle(src_of, dst_of, send, recv, which):
        def go(i, carry):
            peer = lax.rem(me + 1 + i, n)
            copy = pltpu.make_async_remote_copy(
                src_ref=src_of(peer), dst_ref=dst_of(peer), send_sem=send.at[peer], recv_sem=recv.at[peer],
                device_id={"var": peer, "tm": t}, device_id_type=MESH,
            )
            if which == "recv":
                copy.wait_recv()
            else:
                copy.wait_send()
            return carry
        lax.fori_loop(0, n - 1, go, 0)

    def everyone(body):
        def go(i, carry):
            where = lax.rem(my_id + 1 + i, 2 * n)
            body(where, where // 2, lax.rem(where, 2))
            return carry
        lax.fori_loop(0, 2 * n - 1, go, 0)

    barrier = pltpu.get_barrier_semaphore()

    def greet(where, p, q):
        pl.semaphore_signal(barrier, inc=1, device_id={"var": p, "tm": q}, device_id_type=MESH)
    everyone(greet)

    ones = jnp.ones((16, steps), BF16)
    sums = dot(ones, w_embed[...])[:8]
    for s in range(samples):
        x = series[s].astype(F32)
        mean = jnp.mean(x, axis=1, keepdims=True)
        centred = x - mean
        spread_sum = jnp.sum(centred * centred, axis=1, keepdims=True)
        width = w_embed.shape[1]
        pack[s, :rows, :width] = dot(centred.astype(BF16), w_embed[...])
        pack[s, :rows, width:width + 128] = jnp.broadcast_to(mean, (rows, 128))
        pack[s, :rows, width + 128:] = jnp.broadcast_to(spread_sum, (rows, 128))
        pack[s, rows:, :width] = sums
        pack[s, rows:, width:] = jnp.zeros((8, 256), F32)

    pl.semaphore_wait(barrier, 2 * n - 1)
    first = to_pair(0, pack.at[other], got)
    first.start()
    weight_copies = [
        to_pair(1, w_query, wq.at[t]),
        to_pair(2, w_key, wk.at[t]),
        to_pair(3, w_value, wv.at[t]),
        to_pair(4, w_out, wo.at[t]),
        to_pair(5, w_head, wh.at[t]),
        to_pair(6, target.at[other], tg.at[t]),
    ]
    for copy in weight_copies:
        copy.start()
    wq[t] = w_query[...]
    wk[t] = w_key[...]
    wv[t] = w_value[...]
    wo[t] = w_out[...]
    wh[t] = w_head[...]
    tg[t] = target[t]
    first.wait()

    width = w_embed.shape[1]
    mean_a, mean_b = pack[t, :rows, width:width + 1], got[:rows, width:width + 1]
    sq_a, sq_b = pack[t, :rows, width + 128:width + 129], got[:rows, width + 128:width + 129]
    center = (mean_a + mean_b) * 0.5
    half_gap = (mean_a - mean_b) * 0.5
    deviation = jnp.sqrt((sq_a + sq_b) * (1.0 / (2 * steps)) + half_gap * half_gap + EPSILON)
    sums_a, sums_b = pack[t, rows:rows + 1, :width], got[rows:rows + 1, :width]
    hidden = (
        (pack[t, :rows, :width] + got[:rows, :width] + half_gap * (sums_a - sums_b)) / deviation
    ).astype(BF16)
    hid[t, block, :] = hidden

    mine = hid.at[t, block, :]
    hid_from = lambda p: hid.at[t, pl.ds(pl.multiple_of(p * rows, rows), rows), :]
    spread(lambda p: mine, hid_from, hid_send, hid_recv)

    for copy in weight_copies:
        copy.wait()
    queries = jnp.concatenate([dot(hidden, wq[0]), dot(hidden, wq[1])], axis=1).astype(BF16)
    queries = (queries.astype(F32) * HEAD_DIM ** (-0.5)).astype(BF16)
    q_heads = [queries[:, h * HEAD_DIM:(h + 1) * HEAD_DIM] for h in range(heads)]

    settle(lambda p: mine, hid_from, hid_send, hid_recv, "recv")
    relay = to_pair(7, hid.at[t], hid.at[t])
    relay.start()

    chunks = n * rows // key_chunk

    def chunk_rows(c):
        if chunks == 1:
            return pl.ds(0, key_chunk)
        return pl.ds(pl.multiple_of(c * key_chunk, key_chunk), key_chunk)

    def forward(c, carry):
        totals, summed = carry
        at = chunk_rows(c)
        h_rows = hid[t, at, :]
        key_rows = jnp.concatenate([dot(h_rows, wk[0]), dot(h_rows, wk[1])], axis=1).astype(BF16)
        value_rows = jnp.concatenate([dot(h_rows, wv[0]), dot(h_rows, wv[1])], axis=1).astype(BF16)
        keys[at, :] = key_rows
        values[at, :] = value_rows
        new_totals, new_summed = [], []
        for h in range(heads):
            cols = slice(h * HEAD_DIM, (h + 1) * HEAD_DIM)
            p = jnp.exp(dot_nt(q_heads[h], key_rows[:, cols]))
            powers[h, c] = p
            new_totals.append(totals[h] + jnp.sum(p, axis=1, keepdims=True))
            new_summed.append(summed[h] + dot(p.astype(BF16), value_rows[:, cols]))
        return tuple(new_totals), tuple(new_summed)

    zero = (
        tuple(jnp.zeros((rows, 1), F32) for _ in range(heads)),
        tuple(jnp.zeros((rows, HEAD_DIM), F32) for _ in range(heads)),
    )
    totals, summed = repeat(chunks, forward, zero)
    context = jnp.concatenate([summed[h] / totals[h] for h in range(heads)], axis=1)
    context_low = context.astype(BF16)
    half = context.shape[1] // 2
    w_out_all = wo[...].reshape(2 * half, width)
    residual = hidden.astype(F32) + dot(context_low, w_out_all)
    shifted = residual - jnp.mean(residual, axis=1, keepdims=True)
    norm_root = jnp.sqrt(jnp.mean(shifted * shifted, axis=1, keepdims=True) + EPSILON)
    unit_rows = shifted / norm_root
    gain = norm_gain[...]
    normal_out = (unit_rows * gain).astype(BF16)
    no2[t] = normal_out
    send_no = to_pair(8, no2.at[t], no2.at[t])
    send_no.start()
    grad_normal = jnp.zeros((rows, width), F32)
    for h in range(2):
        horizon_norm = dot(normal_out, wh[h])
        pred_half[h] = horizon_norm * deviation + center
        errors = horizon_norm - (tg[h] - center) / deviation
        grad_h = (errors * (2.0 / (samples * horizon))).astype(BF16)
        gh_all[h] = grad_h
        grad_normal += dot_nt(grad_h, wh[h])
    send_gh = to_pair(9, gh_all.at[other], gh2.at[t])
    send_gh.start()
    send_pred = to_pair(10, pred_half.at[other], pred_got)
    send_pred.start()
    gh2[t] = gh_all[t]
    pred_out[t] = pred_half[t]

    gain_mine[...] = jnp.sum(grad_normal * unit_rows, axis=0, keepdims=True)
    grad_unit = grad_normal * gain
    grad_mix = (
        (
            grad_unit
            - jnp.mean(grad_unit, axis=1, keepdims=True)
            - unit_rows * jnp.mean(grad_unit * unit_rows, axis=1, keepdims=True)
        )
        / norm_root
    ).astype(BF16)
    gm2[t] = grad_mix
    for h in range(2):
        cl_all[h] = context_low[:, h * half:(h + 1) * half]
    send_gm = to_pair(11, gm2.at[t], gm2.at[t])
    send_gm.start()
    send_cl = to_pair(12, cl_all.at[other], cl2.at[t])
    send_cl.start()
    cl2[t] = cl_all[t]

    def gain_copy(where, p, q, slot):
        return pltpu.make_async_remote_copy(
            src_ref=gain_mine, dst_ref=gains.at[slot], send_sem=gain_send.at[where], recv_sem=gain_recv.at[slot],
            device_id={"var": p, "tm": q}, device_id_type=MESH,
        )

    if reduce_here:
        gains[my_id] = gain_mine[...]
        everyone(lambda where, p, q: gain_copy(where, p, q, my_id).start())
    else:
        gain_out[...] = gain_mine[...]

    grad_context = dot_nt(grad_mix, w_out_all)
    gc_heads, row_dots, scales = [], [], []
    for h in range(heads):
        cols = slice(h * HEAD_DIM, (h + 1) * HEAD_DIM)
        gc_heads.append(grad_context[:, cols].astype(BF16))
        row_dots.append(jnp.sum(grad_context[:, cols] * context[:, cols], axis=1, keepdims=True))
        scales.append(1.0 / totals[h])

    def backward(c, carry):
        at = chunk_rows(c)
        key_rows, value_rows = keys[at, :], values[at, :]
        results = []
        for h in range(heads):
            cols = slice(h * HEAD_DIM, (h + 1) * HEAD_DIM)
            grad_weights = dot_nt(gc_heads[h], value_rows[:, cols])
            grad_scores = (powers[h, c] * scales[h] * (grad_weights - row_dots[h])).astype(BF16)
            results.append(carry[h] + dot(grad_scores, key_rows[:, cols]))
        return tuple(results)

    grads = repeat(chunks, backward, zero[1])
    grad_query = (jnp.concatenate(grads, axis=1) * HEAD_DIM ** (-0.5)).astype(BF16)
    for h in range(2):
        gq_src[h] = grad_query[:, h * half:(h + 1) * half]

    def gq_copy(where, p, q, slot):
        return pltpu.make_async_remote_copy(
            src_ref=gq_src.at[q],
            dst_ref=gq_all.at[lax.rem(slot, 2), pl.ds(pl.multiple_of((slot // 2) * rows, rows), rows), :],
            send_sem=gq_send.at[where], recv_sem=gq_recv.at[slot],
            device_id={"var": p, "tm": q}, device_id_type=MESH,
        )

    everyone(lambda where, p, q: gq_copy(where, p, q, my_id).start())
    gq_all[t, block, :] = gq_src[t]

    send_no.wait()
    send_gh.wait()
    head_term = dot_tn(no2[...].reshape(samples * rows, width), gh2[...].reshape(samples * rows, horizon // 2))
    if reduce_here:
        head_src[...] = head_term.astype(BF16).reshape(head_src.shape)
        spread(lambda p: head_src.at[p], lambda p: head_slots.at[p], hr_send, hr_recv)
    else:
        head_out[...] = head_term
    send_gm.wait()
    send_cl.wait()
    out_term = dot_tn(cl2[...].reshape(samples * rows, half), gm2[...].reshape(samples * rows, width))
    if reduce_here:
        out_src[...] = out_term.astype(BF16).reshape(out_src.shape)
        spread(lambda p: out_src.at[p], lambda p: out_slots.at[p], or_send, or_recv)
        head_slots[me] = head_src[me]
        out_slots[me] = out_src[me]
    else:
        final_out[...] = out_term
    send_pred.wait()
    pred_out[other] = pred_got[...]

    if reduce_here:
        settle(lambda p: head_src.at[p], lambda p: head_slots.at[p], hr_send, hr_recv, "recv")
        head_full[me] = jnp.sum(head_slots[...].astype(F32), axis=0).astype(BF16)
        spread(lambda p: head_full.at[me], lambda p: head_full.at[p], ha_send, ha_recv)
        settle(lambda p: out_src.at[p], lambda p: out_slots.at[p], or_send, or_recv, "recv")
        out_full[me] = jnp.sum(out_slots[...].astype(F32), axis=0).astype(BF16)
        spread(lambda p: out_full.at[me], lambda p: out_full.at[p], oa_send, oa_recv)

    relay.wait()
    everyone(lambda where, p, q: gq_copy(where, p, q, where).wait_recv())
    query_out[...] = dot_tn(
        hid[...].reshape(samples * n * rows, width), gq_all[...].reshape(samples * n * rows, half)
    )
    if reduce_here:
        everyone(lambda where, p, q: gain_copy(where, p, q, where).wait_recv())
        gain_out[...] = jnp.sum(gains[...], axis=0)
        settle(lambda p: head_full.at[me], lambda p: head_full.at[p], ha_send, ha_recv, "recv")
        head_out[...] = head_full[...].astype(F32).reshape(head_out.shape)
        settle(lambda p: out_full.at[me], lambda p: out_full.at[p], oa_send, oa_recv, "recv")
        final_out[...] = out_full[...].astype(F32).reshape(final_out.shape)

    settle(lambda p: mine, hid_from, hid_send, hid_recv, "send")
    everyone(lambda where, p, q: gq_copy(where, p, q, my_id).wait_send())
    if reduce_here:
        everyone(lambda where, p, q: gain_copy(where, p, q, my_id).wait_send())
        settle(lambda p: head_src.at[p], lambda p: head_slots.at[p], hr_send, hr_recv, "send")
        settle(lambda p: out_src.at[p], lambda p: out_slots.at[p], or_send, or_recv, "send")
        settle(lambda p: head_full.at[me], lambda p: head_full.at[p], ha_send, ha_recv, "send")
        settle(lambda p: out_full.at[me], lambda p: out_full.at[p], oa_send, oa_recv, "send")


def solution(mesh):
    n = mesh.shape["var"]

    def per_device(series, target, w_embed, w_query, w_key, w_value, w_out, norm_gain, w_head):
        samples, rows, steps = series.shape
        width = w_embed.shape[1]
        half = w_query.shape[1]
        hor = target.shape[2]
        heads = 2 * half // HEAD_DIM
        key_chunk = min(512, n * rows)
        chunks = n * rows // key_chunk
        reduce_here = width % (16 * n) == 0 and half % (16 * n) == 0
        cuts = n if reduce_here else 1
        v = pltpu.VMEM
        dma = pltpu.SemaphoreType.DMA
        outs = pl.pallas_call(
            functools.partial(kernel, n, reduce_here, key_chunk),
            out_shape=(
                jax.ShapeDtypeStruct((samples, rows, hor), F32),
                jax.ShapeDtypeStruct((width, half), F32),
                jax.ShapeDtypeStruct((half, width), F32),
                jax.ShapeDtypeStruct((1, width), F32),
                jax.ShapeDtypeStruct((width, hor), F32),
            ),
            in_specs=[pl.BlockSpec(memory_space=pltpu.VMEM)] * 9,
            out_specs=[pl.BlockSpec(memory_space=pltpu.VMEM)] * 5,
            scratch_shapes=[
                v((samples, rows + 8, width + 256), F32),
                v((rows + 8, width + 256), F32),
                v((2, width, half), BF16),
                v((2, width, half), BF16),
                v((2, width, half), BF16),
                v((2, half, width), BF16),
                v((2, width, hor), BF16),
                v((2, rows, hor), F32),
                v((samples, n * rows, width), BF16),
                v((n * rows, 2 * half), BF16),
                v((n * rows, 2 * half), BF16),
                v((heads, chunks, rows, key_chunk), F32),
                v((2, rows, hor), F32),
                v((rows, hor), F32),
                v((samples, rows, width), BF16),
                v((2, rows, hor), BF16),
                v((samples, rows, hor), BF16),
                v((samples, rows, width), BF16),
                v((2, rows, half), BF16),
                v((samples, rows, half), BF16),
                v((2, rows, half), BF16),
                v((samples, n * rows, half), BF16),
                v((2 * cuts, 1, width), F32),
                v((1, width), F32),
                v((cuts, width // cuts, hor), BF16),
                v((cuts, width // cuts, hor), BF16),
                v((cuts, width // cuts, hor), BF16),
                v((cuts, half // cuts, width), BF16),
                v((cuts, half // cuts, width), BF16),
                v((cuts, half // cuts, width), BF16),
                dma((13,)), dma((13,)),
                dma((n,)), dma((n,)),
                dma((2 * n,)), dma((2 * n,)),
                dma((2 * n,)), dma((2 * n,)),
                dma((n,)), dma((n,)), dma((n,)), dma((n,)),
                dma((n,)), dma((n,)), dma((n,)), dma((n,)),
            ],
            compiler_params=pltpu.CompilerParams(
                collective_id=0,
                has_side_effects=True,
                vmem_limit_bytes=(40 if n <= 16 else 62) * 1024 * 1024,
            ),
        )(series, target, w_embed, w_query, w_key, w_value, w_out, norm_gain.reshape(1, width), w_head)
        pred, query, final, gain, head = outs
        if not reduce_here:
            query_same = query
            final, gain, head = lax.psum((final, gain, head), "var")
            gain = lax.psum(gain, "tm")
            query = query_same
        return pred, query, final, gain.reshape(width), head

    in_specs = (
        P("groups", "var", "tm"),
        P("groups", "var", "tm"),
        P("tm", None),
        P(None, "tm"),
        P(None, "tm"),
        P(None, "tm"),
        P("tm", None),
        P(),
        P(None, "tm"),
    )
    out_specs = (
        P("groups", "var", "tm"),
        P("groups", "tm"),
        P(("groups", "tm"), None),
        P("groups"),
        P("groups", "tm"),
    )
    return jax.shard_map(
        per_device, mesh=mesh, in_specs=in_specs, out_specs=out_specs, check_vma=False
    )
```

time: 235 us -> 74.3 us (0.32)
  waiting for transfers between devices: 97.8 us -> 0 us
  blocking collectives: 92.8 us -> 0 us
  Pallas kernels: 0 us -> 60.5 us
  matrix products: 14.4 us -> 0 us
  between operations: 14.1 us -> 0.66 us
  other arithmetic: 7.29 us -> 0 us
  local copies, waits for them, and re-layouts: 7.82 us -> 12.8 us
    psum x3 -> x0, waiting for transfers between devices: 97.7 us -> none  [the longest x1 61.8 us: per_device(): lax.psum((head_term, gain_term, out_term, query_term), 'var')]
    all_gather x2 -> x0, blocking collectives: 63.1 us -> none  [the longest x1 32.3 us: per_device(): lax.all_gather(value_rows, 'var', axis=1, tiled=True)]
    pallas_call x0 -> x1, Pallas kernels: none -> 60.5 us  [per_device(): pl.pallas_call(functools.partial(kernel, n, reduce_here, key_chunk), out_...]
    psum x3 -> x0, blocking collectives: 29.7 us -> none  [the longest x1 22.8 us: per_device(): lax.psum((head_term, gain_term, out_term, query_term), 'var')]
    dot_general x17 -> x0, matrix products: 14.4 us -> none  [the longest x1 2.16 us: per_device(): jnp.einsum('svd,dh->svh', normal_out, w_head, preferred_element_type=jnp....]
    unnamed x39 -> x22, local copies, waits for them, and re-layouts: 6.63 us -> 12.8 us
    reduce_sum x6 -> x0, other arithmetic: 6.19 us -> none  [the longest x1 1.72 us: per_device(): gain_term = jnp.sum(grad_normal * unit_rows, axis=(0, 1))]
  transfers between devices with their start and end apart: 3 -> 0, of which waited for: 3 -> 0; matrix products, arithmetic and copies ran while one was open for 1% -> 0% of each run, Pallas kernels for 0% -> 0%
where the time goes in v1:
time: 74.3 us; the launch traced here: 74 us
  Pallas kernels  60.5 us (81%)
  local copies, waits for them, and re-layouts  12.8 us (17%)
    pallas_call x1, Pallas kernels, per_device(): pl.pallas_call(functools.partial(kernel, n, reduce_here, key_chunk), out_...  60.5 us
    unnamed x22, local copies, waits for them, and re-layouts  12.8 us

profile of v1, /device:TPU:0, one launch (start us, length us, event | category | flops | bytes accessed | tf_op | source)
XLA Modules:
  0.0 74.0 jit_solution(18085004701282554969)
XLA Ops:
  0.6 1.2 %copy.14.w_head = bf16[512,360]{1,0:T(8,128)(2,1)S(1)} copy(bf16[512,360]{0,1:T(8,128)(2,1)} %param.17) | data formatting | bytes 737280 | tf_op args[8]
  1.8 0.0 copy-start
  1.8 1.6 %copy-done = bf16[2048,512]{1,0:T(8,128)(2,1)S(1)} copy-done((bf16[2048,512]{1,0:T(8,128)(2,1)S(1)}, bf16[2048,512]{1,0:T(8,128)(2,1)}, u32[]{:S(2)}) %copy-start) | copy-done | bytes 2097176
  3.4 0.0 copy-start.1
  3.4 1.0 %copy-done.1 = bf16[2,64,2048]{2,1,0:T(8,128)(2,1)S(1)} copy-done((bf16[2,64,2048]{2,1,0:T(8,128)(2,1)S(1)}, bf16[2,64,2048]{2,1,0:T(8,128)(2,1)}, u32[]{:S(2)}) %copy-start.1) | copy-done | bytes 524312
  4.5 0.0 copy-start.2
  4.5 0.9 %copy-done.2 = f32[2,64,360]{2,1,0:T(8,128)S(1)} copy-done((f32[2,64,360]{2,1,0:T(8,128)S(1)}, f32[2,64,360]{2,1,0:T(8,128)}, u32[]{:S(2)}) %copy-start.2) | copy-done | bytes 184344
  5.4 0.0 copy-start.3
  5.4 0.9 %copy-done.3 = bf16[512,128]{1,0:T(8,128)(2,1)S(1)} copy-done((bf16[512,128]{1,0:T(8,128)(2,1)S(1)}, bf16[512,128]{1,0:T(8,128)(2,1)}, u32[]{:S(2)}) %copy-start.3) | copy-done | bytes 131096
  6.3 0.0 copy-start.4
  6.3 0.9 %copy-done.4 = bf16[512,128]{1,0:T(8,128)(2,1)S(1)} copy-done((bf16[512,128]{1,0:T(8,128)(2,1)S(1)}, bf16[512,128]{1,0:T(8,128)(2,1)}, u32[]{:S(2)}) %copy-start.4) | copy-done | bytes 131096
  7.2 0.0 copy-start.5
  7.2 0.9 %copy-done.5 = bf16[512,128]{1,0:T(8,128)(2,1)S(1)} copy-done((bf16[512,128]{1,0:T(8,128)(2,1)S(1)}, bf16[512,128]{1,0:T(8,128)(2,1)}, u32[]{:S(2)}) %copy-start.5) | copy-done | bytes 131096
  8.1 0.0 copy-start.6
  8.1 0.9 %copy-done.6 = bf16[128,512]{1,0:T(8,128)(2,1)S(1)} copy-done((bf16[128,512]{1,0:T(8,128)(2,1)S(1)}, bf16[128,512]{1,0:T(8,128)(2,1)}, u32[]{:S(2)}) %copy-start.6) | copy-done | bytes 131096
  9.0 0.0 copy-start.7
  9.0 0.7 copy-done.7
  9.7 60.5 %shard_map.128 = (f32[2,64,360]{2,1,0:T(8,128)S(1)}, f32[512,128]{1,0:T(8,128)S(1)}, f32[128,512]{1,0:T(8,128)S(1)}, f32[1,512]{1,0:T(1,128)S(1)}, f32[512,360]{1,0:T(8,128)S(1)}) custom-call(bf16[2,64,2048]{2,1,0:T(8,128)(2,1)S(1)} %copy-done.1, f32[2,64,360]{2,1,0:T(8,128)S(1)} %copy-done.2, bf16[2048,512]{1,0:T(8,128)(2,1)S(1)} %copy-done, ...), custom_call_target="tpu_custom_call" | custom-call | tf_op jit(solution)/shard_map/pallas_call | solution.py:350
  70.2 1.1 %copy.15 = f32[512,360]{0,1:T(8,128)} copy(f32[512,360]{1,0:T(8,128)S(1)} %get-tuple-element.19) | data formatting | bytes 1474560
  71.3 0.7 copy.20
  72.0 0.7 copy.21
  72.7 0.7 copy.22
  73.4 0.6 copy.23
Async XLA Ops:
  1.8 1.6 %copy-start = (bf16[2048,512]{1,0:T(8,128)(2,1)S(1)}, bf16[2048,512]{1,0:T(8,128)(2,1)}, u32[]{:S(2)}) copy-start(bf16[2048,512]{1,0:T(8,128)(2,1)} %w_embed.1) | copy-start | bytes 6291460
  3.4 1.0 %copy-start.1 = (bf16[2,64,2048]{2,1,0:T(8,128)(2,1)S(1)}, bf16[2,64,2048]{2,1,0:T(8,128)(2,1)}, u32[]{:S(2)}) copy-start(bf16[2,64,2048]{2,1,0:T(8,128)(2,1)} %series.1) | copy-start | bytes 1572868
  4.5 0.9 %copy-start.2 = (f32[2,64,360]{2,1,0:T(8,128)S(1)}, f32[2,64,360]{2,1,0:T(8,128)}, u32[]{:S(2)}) copy-start(f32[2,64,360]{2,1,0:T(8,128)} %target.1) | copy-start | bytes 552964
  5.4 0.9 %copy-start.3 = (bf16[512,128]{1,0:T(8,128)(2,1)S(1)}, bf16[512,128]{1,0:T(8,128)(2,1)}, u32[]{:S(2)}) copy-start(bf16[512,128]{1,0:T(8,128)(2,1)} %w_query.1) | copy-start | bytes 393220
  6.3 0.9 %copy-start.4 = (bf16[512,128]{1,0:T(8,128)(2,1)S(1)}, bf16[512,128]{1,0:T(8,128)(2,1)}, u32[]{:S(2)}) copy-start(bf16[512,128]{1,0:T(8,128)(2,1)} %w_key.1) | copy-start | bytes 393220
  7.2 0.9 %copy-start.5 = (bf16[512,128]{1,0:T(8,128)(2,1)S(1)}, bf16[512,128]{1,0:T(8,128)(2,1)}, u32[]{:S(2)}) copy-start(bf16[512,128]{1,0:T(8,128)(2,1)} %w_value.1) | copy-start | bytes 393220
  8.1 0.9 %copy-start.6 = (bf16[128,512]{1,0:T(8,128)(2,1)S(1)}, bf16[128,512]{1,0:T(8,128)(2,1)}, u32[]{:S(2)}) copy-start(bf16[128,512]{1,0:T(8,128)(2,1)} %w_out.1) | copy-start | bytes 393220
  9.0 0.7 copy-start.7

commit v2 on v1

--- a/solution.py
+++ b/solution.py
@@ -9,6 +9,7 @@
 
 HEAD_DIM = 64
 EPSILON = 1e-05
+VMEM_GRANT = 65280 * 1024
 MESH = pl.DeviceIdType.MESH
 F32, BF16 = jnp.float32, jnp.bfloat16
 
@@ -40,6 +41,7 @@
     head_src, head_slots, head_full, out_src, out_slots, out_full,
     pair_send, pair_recv, hid_send, hid_recv, gq_send, gq_recv, gain_send, gain_recv,
     hr_send, hr_recv, ha_send, ha_recv, or_send, or_recv, oa_send, oa_recv,
+    inputs, embed, head_term_f, head_near, head_sum, out_term_f, out_near, out_sum, gain_row, load_sem,
 ):
     me = lax.axis_index("var")
     t = lax.axis_index("tm")
@@ -59,29 +61,74 @@
             device_id={"var": me, "tm": other}, device_id_type=MESH,
         )
 
-    def spread(src_of, dst_of, send, recv):
+    lo, hi, n_hi = lax.rem(me, 2), me // 2, n // 2
+    near = hi * 2 + 1 - lo
+
+    def loop(count, body):
         def go(i, carry):
-            peer = lax.rem(me + 1 + i, n)
-            pltpu.make_async_remote_copy(
-                src_ref=src_of(peer), dst_ref=dst_of(me), send_sem=send.at[peer], recv_sem=recv.at[me],
-                device_id={"var": peer, "tm": t}, device_id_type=MESH,
-            ).start()
+            body(i)
             return carry
-        lax.fori_loop(0, n - 1, go, 0)
-
-    def settle(src_of, dst_of, send, recv, which):
-        def go(i, carry):
-            peer = lax.rem(me + 1 + i, n)
-            copy = pltpu.make_async_remote_copy(
-                src_ref=src_of(peer), dst_ref=dst_of(peer), send_sem=send.at[peer], recv_sem=recv.at[peer],
-                device_id={"var": peer, "tm": t}, device_id_type=MESH,
-            )
+        lax.fori_loop(0, count, go, 0)
+
+    def line_peer(i):
+        return lax.rem(hi + 1 + i, n_hi)
+
+    def var_copy(peer, src, dst, send_sem, recv_sem):
+        return pltpu.make_async_remote_copy(
+            src_ref=src, dst_ref=dst, send_sem=send_sem, recv_sem=recv_sem,
+            device_id={"var": peer, "tm": t}, device_id_type=MESH,
+        )
+
+    def spread(at, send, recv):
+        var_copy(near, at(me), at(me), send.at[near], recv.at[me]).start()
+
+        def go(i):
+            peer = line_peer(i) * 2 + lo
+            var_copy(peer, at(me), at(me), send.at[peer], recv.at[me]).start()
+        loop(n_hi - 1, go)
+
+    def forward_blocks(at, send, recv):
+        def go(i):
+            peer = lax.rem(hi + n_hi - 1 - i, n_hi) * 2 + lo
+            var_copy(peer, at(me), at(peer), send.at[peer], recv.at[peer]).wait_recv()
+            var_copy(near, at(peer), at(peer), send.at[peer + 1 - 2 * lo], recv.at[peer]).start()
+        loop(n_hi - 1, go)
+
+    def settle(at, send, recv, which):
+        if which == "recv":
+            def go(i):
+                block_of = i * 2 + 1 - lo
+                var_copy(near, at(me), at(block_of), send.at[near], recv.at[block_of]).wait_recv()
+            loop(n_hi, go)
+        else:
+            def go(i):
+                peer = lax.rem(me + 1 + i, n)
+                var_copy(near, at(me), at(me), send.at[peer], recv.at[me]).wait_send()
+            loop(n - 1, go)
+
+    def near_copy(bf_ref, got_ref, send, recv):
+        return var_copy(near, bf_ref.at[1 - lo], got_ref, send.at[near], recv.at[hi * 2])
+
+    def line_sum(term_ref, got_ref, sum_ref, slots, send, recv):
+        sum_ref[...] = (term_ref[lo] + got_ref[...].astype(F32)).astype(BF16)
+
+        def go(i):
+            peer = line_peer(i)
+            at = peer * 2 + lo
+            var_copy(at, sum_ref.at[peer], slots.at[hi], send.at[at], recv.at[me]).start()
+        loop(n_hi - 1, go)
+        slots[hi] = sum_ref[hi]
+
+    def line_wait(sum_ref, slots, send, recv, which):
+        def go(i):
+            peer = line_peer(i)
+            at = peer * 2 + lo
+            copy = var_copy(at, sum_ref.at[peer], slots.at[peer], send.at[at], recv.at[at])
             if which == "recv":
                 copy.wait_recv()
             else:
                 copy.wait_send()
-            return carry
-        lax.fori_loop(0, n - 1, go, 0)
+        loop(n_hi - 1, go)
 
     def everyone(body):
         def go(i, carry):
@@ -96,19 +143,50 @@
         pl.semaphore_signal(barrier, inc=1, device_id={"var": p, "tm": q}, device_id_type=MESH)
     everyone(greet)
 
-    ones = jnp.ones((16, steps), BF16)
-    sums = dot(ones, w_embed[...])[:8]
+    pieces = 4
+    piece = steps // pieces
+    load_series = [pltpu.make_async_copy(series.at[k], inputs.at[k], load_sem.at[k]) for k in range(samples)]
+    load_embed = [
+        pltpu.make_async_copy(
+            w_embed.at[pl.ds(k * piece, piece), :], embed.at[pl.ds(k * piece, piece), :],
+            load_sem.at[samples + k],
+        )
+        for k in range(pieces)
+    ]
+    base = samples + pieces
+    load_rest = [
+        pltpu.make_async_copy(src, dst, load_sem.at[base + k])
+        for k, (src, dst) in enumerate([
+            (w_query, wq.at[t]), (w_key, wk.at[t]), (w_value, wv.at[t]), (w_out, wo.at[t]),
+            (w_head, wh.at[t]), (target.at[t], tg.at[t]), (norm_gain, gain_row),
+        ])
+    ]
+    for copy in load_series + load_embed + load_rest:
+        copy.start()
+
+    width = w_embed.shape[1]
+    shifts = []
     for s in range(samples):
-        x = series[s].astype(F32)
+        load_series[s].wait()
+        x = inputs[s].astype(F32)
         mean = jnp.mean(x, axis=1, keepdims=True)
         centred = x - mean
         spread_sum = jnp.sum(centred * centred, axis=1, keepdims=True)
-        width = w_embed.shape[1]
-        pack[s, :rows, :width] = dot(centred.astype(BF16), w_embed[...])
         pack[s, :rows, width:width + 128] = jnp.broadcast_to(mean, (rows, 128))
         pack[s, :rows, width + 128:] = jnp.broadcast_to(spread_sum, (rows, 128))
-        pack[s, rows:, :width] = sums
         pack[s, rows:, width:] = jnp.zeros((8, 256), F32)
+        shifts.append(centred.astype(BF16))
+    shifts.append(jnp.ones((16, steps), BF16))
+    left = jnp.concatenate(shifts, axis=0)
+    total = None
+    for k in range(pieces):
+        load_embed[k].wait()
+        cols = slice(k * piece, (k + 1) * piece)
+        part = dot(left[:, cols], embed[cols, :])
+        total = part if total is None else total + part
+    for s in range(samples):
+        pack[s, :rows, :width] = total[s * rows:(s + 1) * rows]
+        pack[s, rows:, :width] = total[samples * rows:samples * rows + 8]
 
     pl.semaphore_wait(barrier, 2 * n - 1)
     first = to_pair(0, pack.at[other], got)
@@ -123,15 +201,8 @@
     ]
     for copy in weight_copies:
         copy.start()
-    wq[t] = w_query[...]
-    wk[t] = w_key[...]
-    wv[t] = w_value[...]
-    wo[t] = w_out[...]
-    wh[t] = w_head[...]
-    tg[t] = target[t]
     first.wait()
 
-    width = w_embed.shape[1]
     mean_a, mean_b = pack[t, :rows, width:width + 1], got[:rows, width:width + 1]
     sq_a, sq_b = pack[t, :rows, width + 128:width + 129], got[:rows, width + 128:width + 129]
     center = (mean_a + mean_b) * 0.5
@@ -143,17 +214,17 @@
     ).astype(BF16)
     hid[t, block, :] = hidden
 
-    mine = hid.at[t, block, :]
     hid_from = lambda p: hid.at[t, pl.ds(pl.multiple_of(p * rows, rows), rows), :]
-    spread(lambda p: mine, hid_from, hid_send, hid_recv)
-
-    for copy in weight_copies:
+    spread(hid_from, hid_send, hid_recv)
+
+    for copy in weight_copies + load_rest:
         copy.wait()
     queries = jnp.concatenate([dot(hidden, wq[0]), dot(hidden, wq[1])], axis=1).astype(BF16)
     queries = (queries.astype(F32) * HEAD_DIM ** (-0.5)).astype(BF16)
     q_heads = [queries[:, h * HEAD_DIM:(h + 1) * HEAD_DIM] for h in range(heads)]
 
-    settle(lambda p: mine, hid_from, hid_send, hid_recv, "recv")
+    forward_blocks(hid_from, hid_send, hid_recv)
+    settle(hid_from, hid_send, hid_recv, "recv")
     relay = to_pair(7, hid.at[t], hid.at[t])
     relay.start()
 
@@ -194,7 +265,7 @@
     shifted = residual - jnp.mean(residual, axis=1, keepdims=True)
     norm_root = jnp.sqrt(jnp.mean(shifted * shifted, axis=1, keepdims=True) + EPSILON)
     unit_rows = shifted / norm_root
-    gain = norm_gain[...]
+    gain = gain_row[...]
     normal_out = (unit_rows * gain).astype(BF16)
     no2[t] = normal_out
     send_no = to_pair(8, no2.at[t], no2.at[t])
@@ -245,6 +316,18 @@
     else:
         gain_out[...] = gain_mine[...]
 
+    send_no.wait()
+    send_gh.wait()
+    head_term = dot_tn(no2[...].reshape(samples * rows, width), gh2[...].reshape(samples * rows, horizon // 2))
+    if reduce_here:
+        by_lo = head_term.reshape(n_hi, 2, width // n, horizon // 2)
+        for k in range(2):
+            head_term_f[k] = by_lo[:, k]
+            head_src[k] = by_lo[:, k].astype(BF16)
+        head_first = near_copy(head_src, head_near, hr_send, hr_recv)
+        head_first.start()
+    else:
+        head_out[...] = head_term
     grad_context = dot_nt(grad_mix, w_out_all)
     gc_heads, row_dots, scales = [], [], []
     for h in range(heads):
@@ -269,67 +352,77 @@
     for h in range(2):
         gq_src[h] = grad_query[:, h * half:(h + 1) * half]
 
-    def gq_copy(where, p, q, slot):
-        return pltpu.make_async_remote_copy(
-            src_ref=gq_src.at[q],
-            dst_ref=gq_all.at[lax.rem(slot, 2), pl.ds(pl.multiple_of((slot // 2) * rows, rows), rows), :],
-            send_sem=gq_send.at[where], recv_sem=gq_recv.at[slot],
-            device_id={"var": p, "tm": q}, device_id_type=MESH,
-        )
-
-    everyone(lambda where, p, q: gq_copy(where, p, q, my_id).start())
+    swap = to_pair(13, gq_src.at[other], gq_all.at[t, block, :])
+    swap.start()
     gq_all[t, block, :] = gq_src[t]
-
-    send_no.wait()
-    send_gh.wait()
-    head_term = dot_tn(no2[...].reshape(samples * rows, width), gh2[...].reshape(samples * rows, horizon // 2))
-    if reduce_here:
-        head_src[...] = head_term.astype(BF16).reshape(head_src.shape)
-        spread(lambda p: head_src.at[p], lambda p: head_slots.at[p], hr_send, hr_recv)
-    else:
-        head_out[...] = head_term
+    gq_from = lambda p: gq_all.at[:, pl.ds(pl.multiple_of(p * rows, rows), rows), :]
+
+    if reduce_here:
+        head_first.wait()
+        line_sum(head_term_f, head_near, head_sum, head_slots, hr_send, hr_recv)
     send_gm.wait()
     send_cl.wait()
     out_term = dot_tn(cl2[...].reshape(samples * rows, half), gm2[...].reshape(samples * rows, width))
-    if reduce_here:
-        out_src[...] = out_term.astype(BF16).reshape(out_src.shape)
-        spread(lambda p: out_src.at[p], lambda p: out_slots.at[p], or_send, or_recv)
-        head_slots[me] = head_src[me]
-        out_slots[me] = out_src[me]
+    swap.wait()
+    spread(gq_from, gq_send, gq_recv)
+    if reduce_here:
+        by_lo = out_term.reshape(n_hi, 2, half // n, width)
+        for k in range(2):
+            out_term_f[k] = by_lo[:, k]
+            out_src[k] = by_lo[:, k].astype(BF16)
+        out_first = near_copy(out_src, out_near, or_send, or_recv)
+        out_first.start()
     else:
         final_out[...] = out_term
     send_pred.wait()
     pred_out[other] = pred_got[...]
-
-    if reduce_here:
-        settle(lambda p: head_src.at[p], lambda p: head_slots.at[p], hr_send, hr_recv, "recv")
+    relay.wait()
+    forward_blocks(gq_from, gq_send, gq_recv)
+    head_from = lambda p: head_full.at[p]
+    out_from = lambda p: out_full.at[p]
+
+    if reduce_here:
+        out_first.wait()
+        line_sum(out_term_f, out_near, out_sum, out_slots, or_send, or_recv)
+        line_wait(head_sum, head_slots, hr_send, hr_recv, "recv")
         head_full[me] = jnp.sum(head_slots[...].astype(F32), axis=0).astype(BF16)
-        spread(lambda p: head_full.at[me], lambda p: head_full.at[p], ha_send, ha_recv)
-        settle(lambda p: out_src.at[p], lambda p: out_slots.at[p], or_send, or_recv, "recv")
+        spread(head_from, ha_send, ha_recv)
+        line_wait(out_sum, out_slots, or_send, or_recv, "recv")
         out_full[me] = jnp.sum(out_slots[...].astype(F32), axis=0).astype(BF16)
-        spread(lambda p: out_full.at[me], lambda p: out_full.at[p], oa_send, oa_recv)
-
-    relay.wait()
-    everyone(lambda where, p, q: gq_copy(where, p, q, where).wait_recv())
+        spread(out_from, oa_send, oa_recv)
+
+    settle(gq_from, gq_send, gq_recv, "recv")
     query_out[...] = dot_tn(
         hid[...].reshape(samples * n * rows, width), gq_all[...].reshape(samples * n * rows, half)
     )
     if reduce_here:
+        forward_blocks(head_from, ha_send, ha_recv)
+        forward_blocks(out_from, oa_send, oa_recv)
         everyone(lambda where, p, q: gain_copy(where, p, q, where).wait_recv())
         gain_out[...] = jnp.sum(gains[...], axis=0)
-        settle(lambda p: head_full.at[me], lambda p: head_full.at[p], ha_send, ha_recv, "recv")
-        head_out[...] = head_full[...].astype(F32).reshape(head_out.shape)
-        settle(lambda p: out_full.at[me], lambda p: out_full.at[p], oa_send, oa_recv, "recv")
+        settle(head_from, ha_send, ha_recv, "recv")
+        head_out[...] = head_full[...].reshape(head_out.shape)
+        settle(out_from, oa_send, oa_recv, "recv")
         final_out[...] = out_full[...].astype(F32).reshape(final_out.shape)
 
-    settle(lambda p: mine, hid_from, hid_send, hid_recv, "send")
-    everyone(lambda where, p, q: gq_copy(where, p, q, my_id).wait_send())
+    settle(hid_from, hid_send, hid_recv, "send")
+    settle(gq_from, gq_send, gq_recv, "send")
     if reduce_here:
         everyone(lambda where, p, q: gain_copy(where, p, q, my_id).wait_send())
-        settle(lambda p: head_src.at[p], lambda p: head_slots.at[p], hr_send, hr_recv, "send")
-        settle(lambda p: out_src.at[p], lambda p: out_slots.at[p], or_send, or_recv, "send")
-        settle(lambda p: head_full.at[me], lambda p: head_full.at[p], ha_send, ha_recv, "send")
-        settle(lambda p: out_full.at[me], lambda p: out_full.at[p], oa_send, oa_recv, "send")
+        line_wait(head_sum, head_slots, hr_send, hr_recv, "send")
+        line_wait(out_sum, out_slots, or_send, or_recv, "send")
+        settle(head_from, ha_send, ha_recv, "send")
+        settle(out_from, oa_send, oa_recv, "send")
+
+
+def deliver(*refs):
+    count = (len(refs) - 1) // 2
+    sems = refs[-1]
+    copies = [pltpu.make_async_copy(refs[k], refs[count + k], sems.at[k]) for k in range(count)]
+    for copy in copies:
+        copy.start()
+    for copy in copies:
+        copy.wait()
 
 
 def solution(mesh):
@@ -345,6 +438,7 @@
         chunks = n * rows // key_chunk
         reduce_here = width % (16 * n) == 0 and half % (16 * n) == 0
         cuts = n if reduce_here else 1
+        line = n // 2 if reduce_here else 1
         v = pltpu.VMEM
         dma = pltpu.SemaphoreType.DMA
         outs = pl.pallas_call(
@@ -354,9 +448,9 @@
                 jax.ShapeDtypeStruct((width, half), F32),
                 jax.ShapeDtypeStruct((half, width), F32),
                 jax.ShapeDtypeStruct((1, width), F32),
-                jax.ShapeDtypeStruct((width, hor), F32),
+                jax.ShapeDtypeStruct((width, hor), BF16 if reduce_here else F32),
             ),
-            in_specs=[pl.BlockSpec(memory_space=pltpu.VMEM)] * 9,
+            in_specs=[pl.BlockSpec(memory_space=pltpu.HBM)] * 8 + [pl.BlockSpec(memory_space=pltpu.VMEM)],
             out_specs=[pl.BlockSpec(memory_space=pltpu.VMEM)] * 5,
             scratch_shapes=[
                 v((samples, rows + 8, width + 256), F32),
@@ -383,32 +477,49 @@
                 v((samples, n * rows, half), BF16),
                 v((2 * cuts, 1, width), F32),
                 v((1, width), F32),
+                v((2, line, width // cuts, hor), BF16),
+                v((line, width // cuts, hor), BF16),
                 v((cuts, width // cuts, hor), BF16),
-                v((cuts, width // cuts, hor), BF16),
-                v((cuts, width // cuts, hor), BF16),
+                v((2, line, half // cuts, width), BF16),
+                v((line, half // cuts, width), BF16),
                 v((cuts, half // cuts, width), BF16),
-                v((cuts, half // cuts, width), BF16),
-                v((cuts, half // cuts, width), BF16),
-                dma((13,)), dma((13,)),
+                dma((14,)), dma((14,)),
                 dma((n,)), dma((n,)),
-                dma((2 * n,)), dma((2 * n,)),
+                dma((n,)), dma((n,)),
                 dma((2 * n,)), dma((2 * n,)),
                 dma((n,)), dma((n,)), dma((n,)), dma((n,)),
                 dma((n,)), dma((n,)), dma((n,)), dma((n,)),
+                v((samples, rows, steps), BF16),
+                v((steps, width), BF16),
+                v((2, line, width // cuts, hor), F32),
+                v((line, width // cuts, hor), BF16),
+                v((line, width // cuts, hor), BF16),
+                v((2, line, half // cuts, width), F32),
+                v((line, half // cuts, width), BF16),
+                v((line, half // cuts, width), BF16),
+                v((1, width), F32),
+                dma((samples + 11,)),
             ],
             compiler_params=pltpu.CompilerParams(
                 collective_id=0,
                 has_side_effects=True,
-                vmem_limit_bytes=(40 if n <= 16 else 62) * 1024 * 1024,
+                vmem_limit_bytes=VMEM_GRANT,
             ),
         )(series, target, w_embed, w_query, w_key, w_value, w_out, norm_gain.reshape(1, width), w_head)
         pred, query, final, gain, head = outs
         if not reduce_here:
-            query_same = query
             final, gain, head = lax.psum((final, gain, head), "var")
             gain = lax.psum(gain, "tm")
-            query = query_same
-        return pred, query, final, gain.reshape(width), head
+            return pred, query, final, gain.reshape(width), head
+        plain = (pred, query, final, gain)
+        pred, query, final, gain = pl.pallas_call(
+            deliver,
+            out_shape=tuple(jax.ShapeDtypeStruct(x.shape, x.dtype) for x in plain),
+            in_specs=[pl.BlockSpec(memory_space=pl.ANY)] * 4,
+            out_specs=[pl.BlockSpec(memory_space=pltpu.HBM)] * 4,
+            scratch_shapes=[dma((4,))],
+        )(*plain)
+        return pred, query, final, gain.reshape(width), head.astype(F32)
 
     in_specs = (
         P("groups", "var", "tm"),

time: 74.3 us -> 79.6 us (1.071)
  Pallas kernels: 60.5 us -> 74.8 us
  local copies, waits for them, and re-layouts: 12.8 us -> 3.93 us
    pallas_call x0 -> x1, Pallas kernels: none -> 23 us  [per_device(): pl.pallas_call(deliver, out_shape=tuple((jax.ShapeDtypeStruct(x.shape, x....]
    unnamed x22 -> x2, local copies, waits for them, and re-layouts: 12.8 us -> 3.93 us
    pallas_call x1, Pallas kernels: 60.5 us -> 51.7 us  [per_device(): pl.pallas_call(functools.partial(kernel, n, reduce_here, key_chunk), out_...]
where the time goes in v2:
time: 79.6 us; the launch traced here: 79.3 us
  Pallas kernels  74.8 us (94%)
  local copies, waits for them, and re-layouts  3.93 us (5%)
    pallas_call x1, Pallas kernels, per_device(): pl.pallas_call(functools.partial(kernel, n, reduce_here, key_chunk), out_...  51.7 us
    pallas_call x1, Pallas kernels, per_device(): pl.pallas_call(deliver, out_shape=tuple((jax.ShapeDtypeStruct(x.shape, x....  23 us
    unnamed x2, local copies, waits for them, and re-layouts  3.93 us

profile of v2, /device:TPU:0, one launch (start us, length us, event | category | flops | bytes accessed | tf_op | source)
XLA Modules:
  0.0 79.3 jit_solution(4310625866039822293)
XLA Ops:
  0.6 1.9 %copy.14.w_head = bf16[512,360]{1,0:T(8,128)(2,1)} copy(bf16[512,360]{0,1:T(8,128)(2,1)} %param.17) | data formatting | bytes 737280 | tf_op args[8]
  2.5 51.7 %shard_map.128 = (f32[2,64,360]{2,1,0:T(8,128)}, f32[512,128]{1,0:T(8,128)}, f32[128,512]{1,0:T(8,128)}, f32[1,512]{1,0:T(1,128)}, bf16[512,360]{1,0:T(8,128)(2,1)}) custom-call(bf16[2,64,2048]{2,1,0:T(8,128)(2,1)} %series.1, f32[2,64,360]{2,1,0:T(8,128)} %target.1, bf16[2048,512]{1,0:T(8,128)(2,1)} %w_embed.1, bf16[512,128]{1,0:T(8,128)(2,1)} %w_query.1, ...), custom_call_target="tpu_custom_call" | custom-call | tf_op jit(solution)/shard_map/pallas_call | solution.py:444
  54.3 23.0 %shard_map.129 = (f32[2,64,360]{2,1,0:T(8,128)}, f32[512,128]{1,0:T(8,128)}, f32[128,512]{1,0:T(8,128)}, f32[1,512]{1,0:T(1,128)}) custom-call(f32[2,64,360]{2,1,0:T(8,128)} %get-tuple-element.14.refs_0_, f32[512,128]{1,0:T(8,128)} %get-tuple-element.15.refs_1_, f32[128,512]{1,0:T(8,128)} %get-tuple-element.16.refs_2_, f32[1,512]{1,0:T(1,128)} %get-tuple-element.17.refs_3_), custom_call_target="tpu_custom_call" | custom-call | tf_op jit(solution)/shard_map/pallas_call | solution.py:515
  77.3 2.0 %copy.15 = f32[512,360]{0,1:T(8,128)} copy(bf16[512,360]{1,0:T(8,128)(2,1)} %get-tuple-element.22) | data formatting | bytes 1105920

commit v3 on v2

--- a/solution.py
+++ b/solution.py
@@ -393,8 +393,8 @@
 
     settle(gq_from, gq_send, gq_recv, "recv")
     query_out[...] = dot_tn(
-        hid[...].reshape(samples * n * rows, width), gq_all[...].reshape(samples * n * rows, half)
-    )
+        gq_all[...].reshape(samples * n * rows, half), hid[...].reshape(samples * n * rows, width)
+    ).T
     if reduce_here:
         forward_blocks(head_from, ha_send, ha_recv)
         forward_blocks(out_from, oa_send, oa_recv)
@@ -416,12 +416,21 @@
 
 
 def deliver(*refs):
-    count = (len(refs) - 1) // 2
-    sems = refs[-1]
-    copies = [pltpu.make_async_copy(refs[k], refs[count + k], sems.at[k]) for k in range(count)]
-    for copy in copies:
+    count = (len(refs) - 4) // 3
+    sources, results, held = refs[:count], refs[count:2 * count], refs[2 * count:3 * count]
+    turned, in_sems, out_sems, turned_sem = refs[3 * count:]
+    arrive = [pltpu.make_async_copy(sources[k], held[k], in_sems.at[k]) for k in range(count)]
+    leave = [pltpu.make_async_copy(held[k], results[k], out_sems.at[k]) for k in range(count - 1)]
+    for copy in arrive:
         copy.start()
-    for copy in copies:
+    for k in range(count - 1):
+        arrive[k].wait()
+        leave[k].start()
+    arrive[count - 1].wait()
+    turned[...] = held[count - 1][...].astype(F32).T
+    last = pltpu.make_async_copy(turned, results[count - 1], turned_sem)
+    last.start()
+    for copy in leave + [last]:
         copy.wait()
 
 
@@ -511,15 +520,19 @@
             final, gain, head = lax.psum((final, gain, head), "var")
             gain = lax.psum(gain, "tm")
             return pred, query, final, gain.reshape(width), head
-        plain = (pred, query, final, gain)
-        pred, query, final, gain = pl.pallas_call(
+        plain = (pred, query, final, gain, head)
+        shapes = [jax.ShapeDtypeStruct(x.shape, x.dtype) for x in plain[:4]]
+        shapes.append(jax.ShapeDtypeStruct((hor, width), F32))
+        pred, query, final, gain, head = pl.pallas_call(
             deliver,
-            out_shape=tuple(jax.ShapeDtypeStruct(x.shape, x.dtype) for x in plain),
-            in_specs=[pl.BlockSpec(memory_space=pl.ANY)] * 4,
-            out_specs=[pl.BlockSpec(memory_space=pltpu.HBM)] * 4,
-            scratch_shapes=[dma((4,))],
+            out_shape=tuple(shapes),
+            in_specs=[pl.BlockSpec(memory_space=pltpu.HBM)] * 5,
+            out_specs=[pl.BlockSpec(memory_space=pltpu.HBM)] * 5,
+            scratch_shapes=[v(x.shape, x.dtype) for x in plain]
+            + [v((hor, width), F32), dma((5,)), dma((4,)), dma(())],
+            compiler_params=pltpu.CompilerParams(vmem_limit_bytes=VMEM_GRANT),
         )(*plain)
-        return pred, query, final, gain.reshape(width), head.astype(F32)
+        return pred, query, final, gain.reshape(width), jnp.transpose(head)
 
     in_specs = (
         P("groups", "var", "tm"),

time: 79.6 us -> 56.6 us (0.71)
  Pallas kernels: 74.8 us -> 53.9 us
  local copies, waits for them, and re-layouts: 3.93 us -> 1.91 us
    pallas_call x1, Pallas kernels: 23 us -> 2.39 us  [per_device(): pl.pallas_call(deliver, out_shape=tuple(shapes), in_specs=[pl.BlockSpec(m...]
    unnamed x2 -> x1, local copies, waits for them, and re-layouts: 3.93 us -> 1.91 us
where the time goes in v3:
time: 56.6 us; the launch traced here: 56.4 us
  Pallas kernels  53.9 us (95%)
  local copies, waits for them, and re-layouts  1.91 us (3%)
  between operations  0.64 us (1%)
    pallas_call x1, Pallas kernels, per_device(): pl.pallas_call(functools.partial(kernel, n, reduce_here, key_chunk), out_...  51.5 us
    pallas_call x1, Pallas kernels, per_device(): pl.pallas_call(deliver, out_shape=tuple(shapes), in_specs=[pl.BlockSpec(m...  2.39 us
    unnamed x1, local copies, waits for them, and re-layouts  1.91 us

profile of v3, /device:TPU:0, one launch (start us, length us, event | category | flops | bytes accessed | tf_op | source)
XLA Modules:
  0.0 56.4 jit_solution(764487373238147292)
XLA Ops:
  0.6 1.9 %copy.14.w_head = bf16[512,360]{1,0:T(8,128)(2,1)} copy(bf16[512,360]{0,1:T(8,128)(2,1)} %param.17) | data formatting | bytes 737280 | tf_op args[8]
  2.5 51.5 %shard_map.128 = (f32[2,64,360]{2,1,0:T(8,128)}, f32[512,128]{1,0:T(8,128)}, f32[128,512]{1,0:T(8,128)}, f32[1,512]{1,0:T(1,128)}, bf16[512,360]{1,0:T(8,128)(2,1)}) custom-call(bf16[2,64,2048]{2,1,0:T(8,128)(2,1)} %series.1, f32[2,64,360]{2,1,0:T(8,128)} %target.1, bf16[2048,512]{1,0:T(8,128)(2,1)} %w_embed.1, bf16[512,128]{1,0:T(8,128)(2,1)} %w_query.1, ...), custom_call_target="tpu_custom_call" | custom-call | tf_op jit(solution)/shard_map/pallas_call | solution.py:453
  54.0 2.4 %shard_map.129 = (f32[2,64,360]{2,1,0:T(8,128)}, f32[512,128]{1,0:T(8,128)}, f32[128,512]{1,0:T(8,128)}, f32[1,512]{1,0:T(1,128)}, f32[360,512]{1,0:T(8,128)}) custom-call(f32[2,64,360]{2,1,0:T(8,128)} %get-tuple-element.15.refs_0_, f32[512,128]{1,0:T(8,128)} %get-tuple-element.16.refs_1_, f32[128,512]{1,0:T(8,128)} %get-tuple-element.17.refs_2_, ...), custom_call_target="tpu_custom_call" | custom-call | tf_op jit(solution)/shard_map/pallas_call | solution.py:526

commit v4 on v3

--- a/solution.py
+++ b/solution.py
@@ -71,7 +71,12 @@
         lax.fori_loop(0, count, go, 0)
 
     def line_peer(i):
-        return lax.rem(hi + 1 + i, n_hi)
+        upper = 2 * hi // n_hi
+        place = hi + upper * (n_hi - 1 - 2 * hi)
+        beyond = (i + n_hi - 2 * place) // n_hi
+        beside = place + (i // 2 + 1) * (1 - 2 * (i % 2))
+        peer = beyond * (i + 1) + (1 - beyond) * beside
+        return peer + upper * (n_hi - 1 - 2 * peer)
 
     def var_copy(peer, src, dst, send_sem, recv_sem):
         return pltpu.make_async_remote_copy(
@@ -89,7 +94,7 @@
 
     def forward_blocks(at, send, recv):
         def go(i):
-            peer = lax.rem(hi + n_hi - 1 - i, n_hi) * 2 + lo
+            peer = line_peer(i) * 2 + lo
             var_copy(peer, at(me), at(peer), send.at[peer], recv.at[peer]).wait_recv()
             var_copy(near, at(peer), at(peer), send.at[peer + 1 - 2 * lo], recv.at[peer]).start()
         loop(n_hi - 1, go)
@@ -217,13 +222,13 @@
     hid_from = lambda p: hid.at[t, pl.ds(pl.multiple_of(p * rows, rows), rows), :]
     spread(hid_from, hid_send, hid_recv)
 
+    forward_blocks(hid_from, hid_send, hid_recv)
     for copy in weight_copies + load_rest:
         copy.wait()
     queries = jnp.concatenate([dot(hidden, wq[0]), dot(hidden, wq[1])], axis=1).astype(BF16)
     queries = (queries.astype(F32) * HEAD_DIM ** (-0.5)).astype(BF16)
     q_heads = [queries[:, h * HEAD_DIM:(h + 1) * HEAD_DIM] for h in range(heads)]
 
-    forward_blocks(hid_from, hid_send, hid_recv)
     settle(hid_from, hid_send, hid_recv, "recv")
     relay = to_pair(7, hid.at[t], hid.at[t])
     relay.start()

time: 56.6 us -> 57.4 us (1.014)
  Pallas kernels: 53.9 us -> 54.7 us
    pallas_call x1, Pallas kernels: 51.5 us -> 52.3 us  [per_device(): pl.pallas_call(functools.partial(kernel, n, reduce_here, key_chunk), out_...]
where the time goes in v4:
time: 57.4 us; the launch traced here: 57.2 us
  Pallas kernels  54.7 us (95%)
  local copies, waits for them, and re-layouts  1.91 us (3%)
  between operations  0.64 us (1%)
    pallas_call x1, Pallas kernels, per_device(): pl.pallas_call(functools.partial(kernel, n, reduce_here, key_chunk), out_...  52.3 us
    pallas_call x1, Pallas kernels, per_device(): pl.pallas_call(deliver, out_shape=tuple(shapes), in_specs=[pl.BlockSpec(m...  2.39 us
    unnamed x1, local copies, waits for them, and re-layouts  1.91 us

profile of v4, /device:TPU:0, one launch (start us, length us, event | category | flops | bytes accessed | tf_op | source)
XLA Modules:
  0.0 57.2 jit_solution(13689181758086478739)
XLA Ops:
  0.6 1.9 %copy.14.w_head = bf16[512,360]{1,0:T(8,128)(2,1)} copy(bf16[512,360]{0,1:T(8,128)(2,1)} %param.17) | data formatting | bytes 737280 | tf_op args[8]
  2.5 52.3 %shard_map.128 = (f32[2,64,360]{2,1,0:T(8,128)}, f32[512,128]{1,0:T(8,128)}, f32[128,512]{1,0:T(8,128)}, f32[1,512]{1,0:T(1,128)}, bf16[512,360]{1,0:T(8,128)(2,1)}) custom-call(bf16[2,64,2048]{2,1,0:T(8,128)(2,1)} %series.1, f32[2,64,360]{2,1,0:T(8,128)} %target.1, bf16[2048,512]{1,0:T(8,128)(2,1)} %w_embed.1, bf16[512,128]{1,0:T(8,128)(2,1)} %w_query.1, ...), custom_call_target="tpu_custom_call" | custom-call | tf_op jit(solution)/shard_map/pallas_call | solution.py:458
  54.8 2.4 %shard_map.129 = (f32[2,64,360]{2,1,0:T(8,128)}, f32[512,128]{1,0:T(8,128)}, f32[128,512]{1,0:T(8,128)}, f32[1,512]{1,0:T(1,128)}, f32[360,512]{1,0:T(8,128)}) custom-call(f32[2,64,360]{2,1,0:T(8,128)} %get-tuple-element.15.refs_0_, f32[512,128]{1,0:T(8,128)} %get-tuple-element.16.refs_1_, f32[128,512]{1,0:T(8,128)} %get-tuple-element.17.refs_2_, ...), custom_call_target="tpu_custom_call" | custom-call | tf_op jit(solution)/shard_map/pallas_call | solution.py:531
